TPU v7x, 32 devices: a whole 2x2x4 slice. The times are simulated.
32 devices in a mesh: head: 4 (over x, core), blk: 8 (over z, y).
Axes of the slice: x: 2, y: 2, z: 4, core: 2. Of those that a mesh axis runs over, the one named last changes fastest.
Arguments:
- queries: bfloat16 [8, 512, 2048], P('blk', 'head'), may hold values from -10 to 10
- keys: bfloat16 [8, 512, 512], P('blk', 'head'), may hold values from -10 to 10
- values: bfloat16 [8, 512, 512], P('blk', 'head'), may hold values from -6 to 6
- position: int32 [8, 512], replicated, may hold values from 0 to 4095, as said below
- segment: int32 [8, 512], replicated, may hold values from 0 to 3, as said below
Outputs:
- attended: bfloat16 [8, 512, 2048], P('blk', 'head')
Inputs may be any that keep to these rules, and one draw needn't show every extreme that they name: Each row b holds two runs of 256 consecutive positions in rising order, first c * 256 onward, then (15 - c) * 256 onward, with c a permutation of the rows; every position appears once. `segment`: documents are runs of consecutive positions; their numbers rise with position, start at 0 and may skip values.
All inputs are finite; a program needn't handle non-finite values.
Results may differ from a plain program's by a relative error of at most 0.007.
Values may be sent and summed in bfloat16 or wider, within the bound.
A program may use at most 128 MiB of HBM per device.

v0:
```python
import math

import jax
import jax.numpy as jnp
from jax import lax
from jax.sharding import PartitionSpec as P

LOCAL_QUERY_HEADS = 16
LOCAL_KV_HEADS = 4
HEAD_SIZE = 128


masked_score = -1e30


def absorb(state, query_heads, query_pos, query_seg, key_heads, value_heads, key_pos, key_seg):
    top_old, total_old, accum_old = state
    scores = jnp.einsum(
        "rkgd,ckd->rkgc", query_heads, key_heads, preferred_element_type=jnp.float32
    ) * HEAD_SIZE ** (-0.5)
    visible = ((query_seg[:, None] == key_seg[None, :]) & (key_pos[None, :] <= query_pos[:, None]))[
        :, None, None, :
    ]
    masked = jnp.where(visible, scores, masked_score)
    top_new = jnp.maximum(top_old, jnp.max(masked, axis=-1))
    weights = jnp.where(visible, jnp.exp(masked - top_new[..., None]), 0.0)
    fade = jnp.exp(top_old - top_new)
    total_new = total_old * fade + jnp.sum(weights, axis=-1)
    mixed = jnp.einsum(
        "rkgc,ckd->rkgd",
        weights.astype(jnp.bfloat16),
        value_heads,
        preferred_element_type=jnp.float32,
    )
    accum_new = accum_old * fade[..., None] + mixed
    return (top_new, total_new, accum_new)


def fresh_state(rows, local_kv_heads, group_local):
    return (
        jnp.full((rows, local_kv_heads, group_local), masked_score, jnp.float32),
        jnp.zeros((rows, local_kv_heads, group_local), jnp.float32),
        jnp.zeros((rows, local_kv_heads, group_local, HEAD_SIZE), jnp.float32),
    )


def local(queries, keys, values, position, segment):
    count_heads = lax.axis_size("head")
    tok_block = position.shape[1]
    hq_local = LOCAL_QUERY_HEADS // count_heads
    repeat_factor = max(1, count_heads // LOCAL_KV_HEADS)
    local_kv_heads = LOCAL_KV_HEADS * repeat_factor // count_heads
    group_local = hq_local // local_kv_heads
    local_tokens = keys.shape[1]
    key_dup = jnp.broadcast_to(
        keys.reshape(1, local_tokens, LOCAL_KV_HEADS, 1, HEAD_SIZE),
        (1, local_tokens, LOCAL_KV_HEADS, repeat_factor, HEAD_SIZE),
    ).reshape(1, local_tokens, LOCAL_KV_HEADS * repeat_factor * HEAD_SIZE)
    value_dup = jnp.broadcast_to(
        values.reshape(1, local_tokens, LOCAL_KV_HEADS, 1, HEAD_SIZE),
        (1, local_tokens, LOCAL_KV_HEADS, repeat_factor, HEAD_SIZE),
    ).reshape(1, local_tokens, LOCAL_KV_HEADS * repeat_factor * HEAD_SIZE)
    query_loc, key_loc, value_loc = (
        lax.all_to_all(queries, "head", split_axis=2, concat_axis=1, tiled=True),
        lax.all_to_all(key_dup, "head", split_axis=2, concat_axis=1, tiled=True),
        lax.all_to_all(value_dup, "head", split_axis=2, concat_axis=1, tiled=True),
    )
    query_heads = query_loc.reshape(tok_block, local_kv_heads, group_local, HEAD_SIZE)
    key_heads = key_loc.reshape(tok_block, local_kv_heads, HEAD_SIZE)
    value_heads = value_loc.reshape(tok_block, local_kv_heads, HEAD_SIZE)
    flat_pos = position.reshape(-1)
    flat_seg = segment.reshape(-1)
    block_index = lax.axis_index("blk")
    my_pos = lax.dynamic_slice_in_dim(flat_pos, block_index * tok_block, tok_block)
    my_seg = lax.dynamic_slice_in_dim(flat_seg, block_index * tok_block, tok_block)
    state = fresh_state(tok_block, local_kv_heads, group_local)
    key_piece = lax.all_gather(key_heads, "blk", axis=0, tiled=True)
    value_piece = lax.all_gather(value_heads, "blk", axis=0, tiled=True)
    rows = key_piece.shape[0]
    stride = math.gcd(rows, tok_block)
    count = rows // stride
    key_blocks = key_piece.reshape(count, stride, local_kv_heads, HEAD_SIZE)
    value_blocks = value_piece.reshape(count, stride, local_kv_heads, HEAD_SIZE)
    pos_blocks = flat_pos.reshape(count, stride)
    seg_blocks = flat_seg.reshape(count, stride)

    def advance(carry, item):
        key_block, value_block, pos_block, seg_block = item
        return (
            absorb(
                carry, query_heads, my_pos, my_seg, key_block, value_block, pos_block, seg_block
            ),
            None,
        )

    state, unused = lax.scan(advance, state, (key_blocks, value_blocks, pos_blocks, seg_blocks))
    top_final, total_final, accum_final = state
    attended_local = (
        (accum_final / total_final[..., None])
        .astype(jnp.bfloat16)
        .reshape(1, tok_block, hq_local * HEAD_SIZE)
    )
    return lax.all_to_all(attended_local, "head", split_axis=1, concat_axis=2, tiled=True)


def solution(mesh):
    return jax.shard_map(
        local,
        mesh=mesh,
        in_specs=(P("blk", "head", None), P("blk", "head", None), P("blk", "head", None), P(), P()),
        out_specs=P("blk", "head", None),
        check_vma=False,
    )
```

profile of v0, /device:TPU:0, one launch (start us, length us, event | category | flops | bytes accessed | tf_op | source)
XLA Modules:
  0.0 199.5 jit_solution(5455732661830073139)
XLA Ops:
  6.5 1.1 copy.36
  7.7 0.5 broadcast.78
  8.2 1.3 reduce.2
  9.6 8.6 %all_to_all.63 = bf16[4,2,8192]{2,1,0:T(2,128)(2,1)S(1)} all-to-all(bf16[4,2,8192]{2,1,0:T(2,128)(2,1)S(1)} %reshape.121), channel_id=1, replica_groups=mesh['head'=4,'blk'=8] {'head'}, dimensions={0} | all-to-all | bytes 262144 | tf_op jit(solution)/shard_map/all_to_all | solution.py:65
  18.2 0.1 reshape.122
  18.4 0.8 copy.37
  19.2 1.1 copy.40
  20.3 1.3 reduce.4
  21.7 7.0 %all_to_all.64 = bf16[4,2,8192]{2,1,0:T(2,128)(2,1)S(1)} all-to-all(bf16[4,2,8192]{2,1,0:T(2,128)(2,1)S(1)} %reshape.125), channel_id=1, replica_groups=mesh['head'=4,'blk'=8] {'head'}, dimensions={0} | all-to-all | bytes 262144 | tf_op jit(solution)/shard_map/all_to_all | solution.py:66
  28.7 0.1 reshape.126
  28.8 0.8 copy.41
  29.6 0.8 copy.38
  30.4 11.5 %reduce.3 = bf16[2048,128]{1,0:T(8,128)(2,1)S(1)} reduce(bf16[2048,1,128]{2,1,0:T(2,128)(2,1)S(1)} %bitcast.124, bf16[]{:T(256)} %broadcast.78), dimensions={1}, to_apply=%bitcast.84.reduce_sub_computation | reduce | bytes 1048578
  41.9 0.9 reshape.123
  42.8 3.7 %all-to-all-start.1 = ((bf16[4,2,32768]{2,1,0:T(2,128)(2,1)}), bf16[4,2,32768]{2,1,0:T(2,128)(2,1)S(1)}, u32[]{:S(2)}, u32[]{:S(2)}) async-start(bf16[4,2,32768]{2,1,0:T(2,128)(2,1)} %reshape.123), calls=%async_computation.1 | async-start | bytes 1048576 | tf_op jit(solution)/shard_map/all_to_all | solution.py:64
  46.5 0.1 dynamic_slice.20
  46.7 8.4 %all-to-all-done.1 = bf16[4,2,32768]{2,1,0:T(2,128)(2,1)S(1)} async-done(((bf16[4,2,32768]{2,1,0:T(2,128)(2,1)}), bf16[4,2,32768]{2,1,0:T(2,128)(2,1)S(1)}, u32[]{:S(2)}, u32[]{:S(2)}) %all-to-all-start.1) | async-done | bytes 524320 | tf_op jit(solution)/shard_map/all_to_all | solution.py:64
  55.1 0.5 reshape.124
  55.7 0.2 copy.39
  55.9 0.1 reshape.111
  56.1 3.7 %all-gather.3.cloned.1.call-done = bf16[4096,1,128]{2,0,1:T(8,128)(2,1)} async-done(((bf16[512,1,128]{2,0,1:T(8,128)(2,1)}), bf16[4096,1,128]{2,0,1:T(8,128)(2,1)}) %all-gather.3.cloned.1.call-update) | async-done | bytes 1048592 | tf_op jit(solution)/shard_map/all_gather | solution.py:77
  59.8 41.1 %all-gather.5.cloned.1.call-done = bf16[4096,1,128]{2,0,1:T(8,128)(2,1)} async-done(((bf16[512,1,128]{2,0,1:T(8,128)(2,1)}), bf16[4096,1,128]{2,0,1:T(8,128)(2,1)}) %all-gather.5.cloned.1.call-update) | async-done | bytes 1048592 | tf_op jit(solution)/shard_map/all_gather | solution.py:78
  100.9 73.3 %while.15 = (s32[]{:T(128)}, f32[512,1,4]{0,2,1:T(4,128)S(1)}, f32[512,1,4]{0,2,1:T(4,128)S(1)}, f32[512,1,4,128]{0,3,2,1:T(8,128)S(1)}, s32[512]{0:T(512)S(1)},...) while((s32[]{:T(128)}, f32[512,1,4]{0,2,1:T(4,128)S(1)}, ...), condition=%wide.region_3.4_spmd.clone, body=%wide.region_0.3_spmd.clone.sunk | while | flops 552087552 | bytes 33440936 | solution.py:96
  100.9 0.3 compare_and_fusion.2
  101.2 3.7 %fusion.33 = (f32[512,4]{0,1:T(4,128)S(1)}, f32[512,512,4]{1,0,2:T(8,128)}) fusion(pred[512,512]{0,1:T(8,128)(4,1)S(1)} %compare_and_fusion.2, bf16[512,1,4,128]{3,0,2,1:T(8,128)(2,1)S(1)} %get-tuple-element.287, bf16[8,512,1,128]{3,1,2,0:T(8,128)(2,1)} %get-tuple-element.286, s32[]{:T(128)} %get-tuple-element.265), kind=kOutput, calls=%fused_computation.2.clone.1 | convolution fusion | flops 271579136 | bytes 5120512 | tf_op jit(solution)/shard_map/while/body/eval_jaxpr/rkgd,ckd->rkgc/dot_general | solution.py:18
  104.9 4.0 %fusion.36 = f32[512,1,4,128]{0,3,2,1:T(8,128)S(1)} fusion(f32[512,512,4]{1,0,2:T(8,128)} %get-tuple-element.250, f32[512,4]{0,1:T(4,128)S(1)} %bitcast.125, pred[512,512]{0,1:T(8,128)(4,1)S(1)} %compare_and_fusion.2, f32[512,1,4,128]{0,3,2,1:T(8,128)S(1)} %get-tuple-element.268, f32[512,4]{0,1:T(4,128)S(1)} %get-tuple-element.251, pred[]{:T(512)S(6)} %compare.3, ...), kind=kOutput, calls=%fused_computation.9.clone.1 | convolution fusion | flops 274464768 | bytes 6701569 | tf_op jit(solution)/shard_map/while/body/eval_jaxpr/rkgc,ckd->rkgd/dot_general | solution.py:29
  108.9 1.0 fusion.35
  110.0 0.3 compare_and_fusion.2
  110.3 3.7 %fusion.33 = (f32[512,4]{0,1:T(4,128)S(1)}, f32[512,512,4]{1,0,2:T(8,128)}) fusion(pred[512,512]{0,1:T(8,128)(4,1)S(1)} %compare_and_fusion.2, bf16[512,1,4,128]{3,0,2,1:T(8,128)(2,1)S(1)} %get-tuple-element.287, bf16[8,512,1,128]{3,1,2,0:T(8,128)(2,1)} %get-tuple-element.286, s32[]{:T(128)} %get-tuple-element.265), kind=kOutput, calls=%fused_computation.2.clone.1 | convolution fusion | flops 271579136 | bytes 5120512 | tf_op jit(solution)/shard_map/while/body/eval_jaxpr/rkgd,ckd->rkgc/dot_general | solution.py:18
  114.0 4.0 %fusion.36 = f32[512,1,4,128]{0,3,2,1:T(8,128)S(1)} fusion(f32[512,512,4]{1,0,2:T(8,128)} %get-tuple-element.250, f32[512,4]{0,1:T(4,128)S(1)} %bitcast.125, pred[512,512]{0,1:T(8,128)(4,1)S(1)} %compare_and_fusion.2, f32[512,1,4,128]{0,3,2,1:T(8,128)S(1)} %get-tuple-element.268, f32[512,4]{0,1:T(4,128)S(1)} %get-tuple-element.251, pred[]{:T(512)S(6)} %compare.3, ...), kind=kOutput, calls=%fused_computation.9.clone.1 | convolution fusion | flops 274464768 | bytes 6701569 | tf_op jit(solution)/shard_map/while/body/eval_jaxpr/rkgc,ckd->rkgd/dot_general | solution.py:29
  118.1 1.0 fusion.35
  119.2 0.3 compare_and_fusion.2
  119.5 3.7 %fusion.33 = (f32[512,4]{0,1:T(4,128)S(1)}, f32[512,512,4]{1,0,2:T(8,128)}) fusion(pred[512,512]{0,1:T(8,128)(4,1)S(1)} %compare_and_fusion.2, bf16[512,1,4,128]{3,0,2,1:T(8,128)(2,1)S(1)} %get-tuple-element.287, bf16[8,512,1,128]{3,1,2,0:T(8,128)(2,1)} %get-tuple-element.286, s32[]{:T(128)} %get-tuple-element.265), kind=kOutput, calls=%fused_computation.2.clone.1 | convolution fusion | flops 271579136 | bytes 5120512 | tf_op jit(solution)/shard_map/while/body/eval_jaxpr/rkgd,ckd->rkgc/dot_general | solution.py:18
  123.2 4.0 %fusion.36 = f32[512,1,4,128]{0,3,2,1:T(8,128)S(1)} fusion(f32[512,512,4]{1,0,2:T(8,128)} %get-tuple-element.250, f32[512,4]{0,1:T(4,128)S(1)} %bitcast.125, pred[512,512]{0,1:T(8,128)(4,1)S(1)} %compare_and_fusion.2, f32[512,1,4,128]{0,3,2,1:T(8,128)S(1)} %get-tuple-element.268, f32[512,4]{0,1:T(4,128)S(1)} %get-tuple-element.251, pred[]{:T(512)S(6)} %compare.3, ...), kind=kOutput, calls=%fused_computation.9.clone.1 | convolution fusion | flops 274464768 | bytes 6701569 | tf_op jit(solution)/shard_map/while/body/eval_jaxpr/rkgc,ckd->rkgd/dot_general | solution.py:29
  127.2 1.0 fusion.35
  128.4 0.3 compare_and_fusion.2
  128.6 3.7 %fusion.33 = (f32[512,4]{0,1:T(4,128)S(1)}, f32[512,512,4]{1,0,2:T(8,128)}) fusion(pred[512,512]{0,1:T(8,128)(4,1)S(1)} %compare_and_fusion.2, bf16[512,1,4,128]{3,0,2,1:T(8,128)(2,1)S(1)} %get-tuple-element.287, bf16[8,512,1,128]{3,1,2,0:T(8,128)(2,1)} %get-tuple-element.286, s32[]{:T(128)} %get-tuple-element.265), kind=kOutput, calls=%fused_computation.2.clone.1 | convolution fusion | flops 271579136 | bytes 5120512 | tf_op jit(solution)/shard_map/while/body/eval_jaxpr/rkgd,ckd->rkgc/dot_general | solution.py:18
  132.4 4.0 %fusion.36 = f32[512,1,4,128]{0,3,2,1:T(8,128)S(1)} fusion(f32[512,512,4]{1,0,2:T(8,128)} %get-tuple-element.250, f32[512,4]{0,1:T(4,128)S(1)} %bitcast.125, pred[512,512]{0,1:T(8,128)(4,1)S(1)} %compare_and_fusion.2, f32[512,1,4,128]{0,3,2,1:T(8,128)S(1)} %get-tuple-element.268, f32[512,4]{0,1:T(4,128)S(1)} %get-tuple-element.251, pred[]{:T(512)S(6)} %compare.3, ...), kind=kOutput, calls=%fused_computation.9.clone.1 | convolution fusion | flops 274464768 | bytes 6701569 | tf_op jit(solution)/shard_map/while/body/eval_jaxpr/rkgc,ckd->rkgd/dot_general | solution.py:29
  136.4 1.0 fusion.35
  137.5 0.3 compare_and_fusion.2
  137.8 3.7 %fusion.33 = (f32[512,4]{0,1:T(4,128)S(1)}, f32[512,512,4]{1,0,2:T(8,128)}) fusion(pred[512,512]{0,1:T(8,128)(4,1)S(1)} %compare_and_fusion.2, bf16[512,1,4,128]{3,0,2,1:T(8,128)(2,1)S(1)} %get-tuple-element.287, bf16[8,512,1,128]{3,1,2,0:T(8,128)(2,1)} %get-tuple-element.286, s32[]{:T(128)} %get-tuple-element.265), kind=kOutput, calls=%fused_computation.2.clone.1 | convolution fusion | flops 271579136 | bytes 5120512 | tf_op jit(solution)/shard_map/while/body/eval_jaxpr/rkgd,ckd->rkgc/dot_general | solution.py:18
  141.5 4.0 %fusion.36 = f32[512,1,4,128]{0,3,2,1:T(8,128)S(1)} fusion(f32[512,512,4]{1,0,2:T(8,128)} %get-tuple-element.250, f32[512,4]{0,1:T(4,128)S(1)} %bitcast.125, pred[512,512]{0,1:T(8,128)(4,1)S(1)} %compare_and_fusion.2, f32[512,1,4,128]{0,3,2,1:T(8,128)S(1)} %get-tuple-element.268, f32[512,4]{0,1:T(4,128)S(1)} %get-tuple-element.251, pred[]{:T(512)S(6)} %compare.3, ...), kind=kOutput, calls=%fused_computation.9.clone.1 | convolution fusion | flops 274464768 | bytes 6701569 | tf_op jit(solution)/shard_map/while/body/eval_jaxpr/rkgc,ckd->rkgd/dot_general | solution.py:29
  145.6 1.0 fusion.35
  146.7 0.3 compare_and_fusion.2
  147.0 3.7 %fusion.33 = (f32[512,4]{0,1:T(4,128)S(1)}, f32[512,512,4]{1,0,2:T(8,128)}) fusion(pred[512,512]{0,1:T(8,128)(4,1)S(1)} %compare_and_fusion.2, bf16[512,1,4,128]{3,0,2,1:T(8,128)(2,1)S(1)} %get-tuple-element.287, bf16[8,512,1,128]{3,1,2,0:T(8,128)(2,1)} %get-tuple-element.286, s32[]{:T(128)} %get-tuple-element.265), kind=kOutput, calls=%fused_computation.2.clone.1 | convolution fusion | flops 271579136 | bytes 5120512 | tf_op jit(solution)/shard_map/while/body/eval_jaxpr/rkgd,ckd->rkgc/dot_general | solution.py:18
  150.7 4.0 %fusion.36 = f32[512,1,4,128]{0,3,2,1:T(8,128)S(1)} fusion(f32[512,512,4]{1,0,2:T(8,128)} %get-tuple-element.250, f32[512,4]{0,1:T(4,128)S(1)} %bitcast.125, pred[512,512]{0,1:T(8,128)(4,1)S(1)} %compare_and_fusion.2, f32[512,1,4,128]{0,3,2,1:T(8,128)S(1)} %get-tuple-element.268, f32[512,4]{0,1:T(4,128)S(1)} %get-tuple-element.251, pred[]{:T(512)S(6)} %compare.3, ...), kind=kOutput, calls=%fused_computation.9.clone.1 | convolution fusion | flops 274464768 | bytes 6701569 | tf_op jit(solution)/shard_map/while/body/eval_jaxpr/rkgc,ckd->rkgd/dot_general | solution.py:29
  154.7 1.0 fusion.35
  155.8 0.3 compare_and_fusion.2
  156.1 3.7 %fusion.33 = (f32[512,4]{0,1:T(4,128)S(1)}, f32[512,512,4]{1,0,2:T(8,128)}) fusion(pred[512,512]{0,1:T(8,128)(4,1)S(1)} %compare_and_fusion.2, bf16[512,1,4,128]{3,0,2,1:T(8,128)(2,1)S(1)} %get-tuple-element.287, bf16[8,512,1,128]{3,1,2,0:T(8,128)(2,1)} %get-tuple-element.286, s32[]{:T(128)} %get-tuple-element.265), kind=kOutput, calls=%fused_computation.2.clone.1 | convolution fusion | flops 271579136 | bytes 5120512 | tf_op jit(solution)/shard_map/while/body/eval_jaxpr/rkgd,ckd->rkgc/dot_general | solution.py:18
  159.9 4.0 %fusion.36 = f32[512,1,4,128]{0,3,2,1:T(8,128)S(1)} fusion(f32[512,512,4]{1,0,2:T(8,128)} %get-tuple-element.250, f32[512,4]{0,1:T(4,128)S(1)} %bitcast.125, pred[512,512]{0,1:T(8,128)(4,1)S(1)} %compare_and_fusion.2, f32[512,1,4,128]{0,3,2,1:T(8,128)S(1)} %get-tuple-element.268, f32[512,4]{0,1:T(4,128)S(1)} %get-tuple-element.251, pred[]{:T(512)S(6)} %compare.3, ...), kind=kOutput, calls=%fused_computation.9.clone.1 | convolution fusion | flops 274464768 | bytes 6701569 | tf_op jit(solution)/shard_map/while/body/eval_jaxpr/rkgc,ckd->rkgd/dot_general | solution.py:29
  163.9 1.0 fusion.35
  165.0 0.3 compare_and_fusion.2
  165.3 3.7 %fusion.33 = (f32[512,4]{0,1:T(4,128)S(1)}, f32[512,512,4]{1,0,2:T(8,128)}) fusion(pred[512,512]{0,1:T(8,128)(4,1)S(1)} %compare_and_fusion.2, bf16[512,1,4,128]{3,0,2,1:T(8,128)(2,1)S(1)} %get-tuple-element.287, bf16[8,512,1,128]{3,1,2,0:T(8,128)(2,1)} %get-tuple-element.286, s32[]{:T(128)} %get-tuple-element.265), kind=kOutput, calls=%fused_computation.2.clone.1 | convolution fusion | flops 271579136 | bytes 5120512 | tf_op jit(solution)/shard_map/while/body/eval_jaxpr/rkgd,ckd->rkgc/dot_general | solution.py:18
  169.0 4.0 %fusion.36 = f32[512,1,4,128]{0,3,2,1:T(8,128)S(1)} fusion(f32[512,512,4]{1,0,2:T(8,128)} %get-tuple-element.250, f32[512,4]{0,1:T(4,128)S(1)} %bitcast.125, pred[512,512]{0,1:T(8,128)(4,1)S(1)} %compare_and_fusion.2, f32[512,1,4,128]{0,3,2,1:T(8,128)S(1)} %get-tuple-element.268, f32[512,4]{0,1:T(4,128)S(1)} %get-tuple-element.251, pred[]{:T(512)S(6)} %compare.3, ...), kind=kOutput, calls=%fused_computation.9.clone.1 | convolution fusion | flops 274464768 | bytes 6701569 | tf_op jit(solution)/shard_map/while/body/eval_jaxpr/rkgc,ckd->rkgd/dot_general | solution.py:29
  173.1 1.0 fusion.35
  174.1 0.1 divide_convert_fusion
  174.3 0.9 copy.45
  175.2 3.7 %reduce.5 = bf16[512,512]{1,0:T(8,128)(2,1)S(1)} reduce(bf16[512,1,512]{2,1,0:T(2,128)(2,1)S(1)} %bitcast.123, bf16[]{:T(256)} %broadcast.78), dimensions={1}, to_apply=%bitcast.88.reduce_sub_computation | reduce | bytes 1048578
  178.9 0.4 reshape.127
  179.3 11.4 %all_to_all.65 = bf16[4,2,32768]{2,1,0:T(2,128)(2,1)S(1)} all-to-all(bf16[4,2,32768]{2,1,0:T(2,128)(2,1)S(1)} %reshape.127), channel_id=1, replica_groups=mesh['head'=4,'blk'=8] {'head'}, dimensions={0} | all-to-all | bytes 1048576 | tf_op jit(solution)/shard_map/all_to_all | solution.py:103
  190.7 0.5 reshape.128
  191.2 0.1 copy.53
  191.4 0.3 copy.46
  191.6 1.0 copy.47
  (70 shorter events, 0.8 us)
Async XLA Ops:
  6.5 23.1 %copy-start.1 = (bf16[1,128,2048]{2,1,0:T(8,128)(2,1)S(1)}, bf16[1,128,2048]{2,1,0:T(8,128)(2,1)}, u32[]{:S(2)}) copy-start(bf16[1,128,2048]{2,1,0:T(8,128)(2,1)} %param.7) | copy-start | bytes 1572868
  6.5 53.3 %all-gather.3.cloned.1.call-start = ((), (), s32[]{:S(2)}) async-start(), calls=%async_computation.4 | async-start | bytes 1179648 | tf_op jit(solution)/shard_map/all_gather | solution.py:77
  18.3 28.2 %copy-start.2 = (s32[8,512]{1,0:T(8,128)S(1)}, s32[8,512]{1,0:T(8,128)}, u32[]{:S(2)}) copy-start(s32[8,512]{1,0:T(8,128)} %param.11) | copy-start | bytes 49156
  18.4 28.1 %copy-start.3 = (s32[8,512]{1,0:T(8,128)S(1)}, s32[8,512]{1,0:T(8,128)}, u32[]{:S(2)}) copy-start(s32[8,512]{1,0:T(8,128)} %param.10) | copy-start | bytes 49156
  19.2 81.7 %all-gather.5.cloned.1.call-start = ((), (), s32[]{:S(2)}) async-start(), calls=%async_computation.5 | async-start | bytes 1179648 | tf_op jit(solution)/shard_map/all_gather | solution.py:78
  42.8 12.3 %all-to-all-start.1 = ((bf16[4,2,32768]{2,1,0:T(2,128)(2,1)}), bf16[4,2,32768]{2,1,0:T(2,128)(2,1)S(1)}, u32[]{:S(2)}, u32[]{:S(2)}) async-start(bf16[4,2,32768]{2,1,0:T(2,128)(2,1)} %reshape.123), calls=%async_computation.1 | async-start | bytes 1048576 | tf_op jit(solution)/shard_map/all_to_all | solution.py:64
  104.9 4.0 %copy-start = (f32[512,512,4]{1,0,2:T(8,128)S(1)}, f32[512,512,4]{1,0,2:T(8,128)}, u32[]{:S(2)}) copy-start(f32[512,512,4]{1,0,2:T(8,128)} %get-tuple-element.250) | copy-start | bytes 12582916 | tf_op jit(solution)/shard_map/while
  114.0 4.0 %copy-start = (f32[512,512,4]{1,0,2:T(8,128)S(1)}, f32[512,512,4]{1,0,2:T(8,128)}, u32[]{:S(2)}) copy-start(f32[512,512,4]{1,0,2:T(8,128)} %get-tuple-element.250) | copy-start | bytes 12582916 | tf_op jit(solution)/shard_map/while
  123.2 4.0 %copy-start = (f32[512,512,4]{1,0,2:T(8,128)S(1)}, f32[512,512,4]{1,0,2:T(8,128)}, u32[]{:S(2)}) copy-start(f32[512,512,4]{1,0,2:T(8,128)} %get-tuple-element.250) | copy-start | bytes 12582916 | tf_op jit(solution)/shard_map/while
  132.4 4.0 %copy-start = (f32[512,512,4]{1,0,2:T(8,128)S(1)}, f32[512,512,4]{1,0,2:T(8,128)}, u32[]{:S(2)}) copy-start(f32[512,512,4]{1,0,2:T(8,128)} %get-tuple-element.250) | copy-start | bytes 12582916 | tf_op jit(solution)/shard_map/while
  141.5 4.0 %copy-start = (f32[512,512,4]{1,0,2:T(8,128)S(1)}, f32[512,512,4]{1,0,2:T(8,128)}, u32[]{:S(2)}) copy-start(f32[512,512,4]{1,0,2:T(8,128)} %get-tuple-element.250) | copy-start | bytes 12582916 | tf_op jit(solution)/shard_map/while
  150.7 4.0 %copy-start = (f32[512,512,4]{1,0,2:T(8,128)S(1)}, f32[512,512,4]{1,0,2:T(8,128)}, u32[]{:S(2)}) copy-start(f32[512,512,4]{1,0,2:T(8,128)} %get-tuple-element.250) | copy-start | bytes 12582916 | tf_op jit(solution)/shard_map/while
  159.8 4.0 %copy-start = (f32[512,512,4]{1,0,2:T(8,128)S(1)}, f32[512,512,4]{1,0,2:T(8,128)}, u32[]{:S(2)}) copy-start(f32[512,512,4]{1,0,2:T(8,128)} %get-tuple-element.250) | copy-start | bytes 12582916 | tf_op jit(solution)/shard_map/while
  169.0 4.0 %copy-start = (f32[512,512,4]{1,0,2:T(8,128)S(1)}, f32[512,512,4]{1,0,2:T(8,128)}, u32[]{:S(2)}) copy-start(f32[512,512,4]{1,0,2:T(8,128)} %get-tuple-element.250) | copy-start | bytes 12582916 | tf_op jit(solution)/shard_map/while
Sparse Core Ops, SparseCore 0:
  19.3 40.4 all-gather.2
  61.9 38.8 all-gather.4
where the time goes:
time: 200 us; the launch traced here: 199 us
  matrix products  61.8 us (31%)
  waiting for transfers between devices  53.2 us (27%)
  other arithmetic  28.9 us (14%)
  blocking collectives  27.1 us (14%)
  between operations  13.7 us (7%)
  local copies, waits for them, and re-layouts  10.8 us (5%)
  starting transfers between devices  3.7 us (2%)
    all_gather x1, waiting for transfers between devices, local(): value_piece = lax.all_gather(value_heads, 'blk', axis=0, tiled=True)  41.1 us
    dot_general x8, matrix products, absorb(): jnp.einsum('rkgc,ckd->rkgd', weights.astype(jnp.bfloat16), value_heads, p...  32.2 us
    dot_general x8, matrix products, absorb(): jnp.einsum('rkgd,ckd->rkgc', query_heads, key_heads, preferred_element_ty...  29.6 us
    unnamed x7, other arithmetic  17.9 us
    all_to_all x1, blocking collectives, local(): lax.all_to_all(attended_local, 'head', split_axis=1, concat_axis=2, tiled...  11.4 us
    all_to_all x1, blocking collectives, local(): lax.all_to_all(key_dup, 'head', split_axis=2, concat_axis=1, tiled=True)  8.64 us
    all_to_all x1, waiting for transfers between devices, local(): lax.all_to_all(queries, 'head', split_axis=2, concat_axis=1, tiled=True)  8.39 us
    reduce_sum x8, other arithmetic, absorb(): total_new = total_old * fade + jnp.sum(weights, axis=-1)  8.38 us
  transfers between devices with their start and end apart: 3, of which 3 were waited for; matrix products, arithmetic and copies ran while one was open for 9% of the time, Pallas kernels for 0%

commit v1 on v0

v1 whole, which is shorter than its diff:
```python
import functools
import math

import jax
import jax.numpy as jnp
from jax import lax
from jax.experimental import pallas as pl
from jax.experimental.pallas import tpu as pltpu
from jax.sharding import PartitionSpec as P

QUERY_HEADS = 16
KV_HEADS = 4
HEAD_SIZE = 128
MASKED = -1e30
SCALE = math.log2(math.e) / math.sqrt(HEAD_SIZE)
MESH = pl.DeviceIdType.MESH


def kernel(H, B, q_in, k_in, v_in, pos_ref, seg_ref, out_ref,
           qbuf, kv, segc, obuf, top, total, acc,
           first_send, q_recv, row_recv, sib_recv, fwd_send, sib_send, out_send, out_recv):
    Y = 2 * KV_HEADS // H
    Z = B // Y
    HQ = QUERY_HEADS // H
    HH = H // 2
    T = q_in.shape[0]
    R = qbuf.shape[1]
    width = HQ * HEAD_SIZE
    h = lax.axis_index("head")
    b = lax.axis_index("blk")
    chip, t = h // 2, h % 2
    z, y = b // Y, b % Y
    kv_head = chip * Y + y
    sibling = chip * 2 + 1 - t
    row_me = z * Y + t % Y

    barrier = pltpu.get_barrier_semaphore()
    for i in range(H):
        for r in range(Y):
            @pl.when(jnp.logical_or(h != i, y != r))
            def _():
                pl.semaphore_signal(barrier, inc=1, device_id={"head": i, "blk": z * Y + r}, device_id_type=MESH)

    @pl.when(z > 0)
    def _():
        pl.semaphore_signal(barrier, inc=1, device_id={"head": h, "blk": b - Y}, device_id_type=MESH)

    @pl.when(z < Z - 1)
    def _():
        pl.semaphore_signal(barrier, inc=1, device_id={"head": h, "blk": b + Y}, device_id_type=MESH)

    near = (z > 0).astype(jnp.int32) + (z < Z - 1).astype(jnp.int32)
    pl.semaphore_wait(barrier, H * Y - 1 + near)

    def part(i):
        return i // HH, pl.ds(pl.multiple_of((i % HH) * T, T), T)

    my_half, my_rows = part(h)

    def send(src, dst, send_sem, recv_sem, head, blk, may_be_me, wait=False):
        def remote():
            copy = pltpu.make_async_remote_copy(
                src_ref=src, dst_ref=dst, send_sem=send_sem, recv_sem=recv_sem,
                device_id={"head": head, "blk": blk}, device_id_type=MESH)
            copy.wait_send() if wait else copy.start()

        if not may_be_me:
            remote()
            return
        other = jnp.logical_or(head != h, blk != b)
        pl.when(other)(remote)
        if not wait:
            @pl.when(jnp.logical_not(other))
            def _():
                pltpu.make_async_copy(src, dst, recv_sem).start()

    def exchange(wait):
        for n, array in enumerate((k_in, v_in)):
            for d in range(KV_HEADS):
                d = (d + 1) % KV_HEADS
                k = (kv_head + d) % KV_HEADS
                cols = pl.ds(pl.multiple_of(k * HEAD_SIZE, HEAD_SIZE), HEAD_SIZE)
                send(array.at[:, cols], kv.at[n, b, my_half, my_rows, :],
                     first_send.at[n, d], row_recv.at[b],
                     (k // Y) * 2 + n, z * Y + k % Y, d == 0, wait)
        for half in range(2 // Y):
            for d in range(KV_HEADS):
                d = (d + 1) % KV_HEADS
                k = (kv_head + d) % KV_HEADS
                cols = pl.ds(pl.multiple_of((k * (2 // Y) + half) * width, width), width)
                core = half if Y == 1 else y
                send(q_in.at[:, cols], qbuf.at[my_half, my_rows, :],
                     first_send.at[2 + half, d], q_recv,
                     (k // Y) * 2 + core, z * Y + k % Y, d == 0, wait)

    exchange(False)

    def column(row, c):
        line = seg_ref[pl.ds(row, 1), :].astype(jnp.float32)
        segc[row] = jnp.transpose(jnp.broadcast_to(line, (HEAD_SIZE, 2 * R))).reshape(2, R, HEAD_SIZE)
        return c

    lax.fori_loop(0, B, column, 0)

    def wait_row(row):
        pltpu.make_async_copy(kv.at[t, row], kv.at[t, row], row_recv.at[row]).wait()

    def wait_sibling(row):
        pltpu.make_async_copy(kv.at[1 - t, row], kv.at[1 - t, row], sib_recv.at[row]).wait()

    def pass_on(row, wait=False):
        def copy(head, blk, send_sem, recv_sem):
            c = pltpu.make_async_remote_copy(
                src_ref=kv.at[t, row], dst_ref=kv.at[t, row], send_sem=send_sem, recv_sem=recv_sem,
                device_id={"head": head, "blk": blk}, device_id_type=MESH)
            c.wait_send() if wait else c.start()

        j = row // Y

        @pl.when(jnp.logical_and(j <= z, z < Z - 1))
        def _():
            copy(h, b + Y, fwd_send.at[0, row], row_recv.at[row])

        @pl.when(jnp.logical_and(j >= z, z > 0))
        def _():
            copy(h, b - Y, fwd_send.at[1, row], row_recv.at[row])

        copy(sibling, b, sib_send.at[row], sib_recv.at[row])

    def scores(g, q_half, keys, visible):
        q = qbuf[q_half, :, g * HEAD_SIZE:(g + 1) * HEAD_SIZE]
        s = lax.dot_general(keys, q, (((1,), (1,)), ((), ())), preferred_element_type=jnp.float32)
        return jnp.where(visible, s, MASKED)

    def seg_line(q_half):
        line = seg_ref[pl.ds(row_me, 1), :].astype(jnp.float32)
        return line[:, q_half * R:(q_half + 1) * R]

    def mask(col, line):
        return jnp.concatenate([col] * (R // HEAD_SIZE), axis=1) == line

    def update(g, which, q_half, keys, values_t, visible):
        s = scores(g, q_half, keys, visible)
        top_old = top[which, g]
        top_new = jnp.maximum(top_old, jnp.max(s, axis=0, keepdims=True))
        w = jnp.exp2((s - top_new) * SCALE)
        fade = jnp.exp2((top_old - top_new) * SCALE)
        tot = total[which, g] * fade + jnp.sum(w, axis=0, keepdims=True)
        a = acc[which, g] * fade + jnp.dot(values_t, w.astype(jnp.bfloat16), preferred_element_type=jnp.float32)
        return top_new, tot, a

    def own():
        rows = lax.broadcasted_iota(jnp.int32, (R, R), 0)
        columns = lax.broadcasted_iota(jnp.int32, (R, R), 1)
        for half in range(2):
            keys = kv[0, row_me, half]
            values_t = jnp.transpose(kv[1, row_me, half])
            visible = jnp.logical_and(mask(segc[row_me, half], seg_line(half)), rows <= columns)
            for g in range(HQ):
                s = scores(g, half, keys, visible)
                t_new = jnp.max(s, axis=0, keepdims=True)
                w = jnp.exp2((s - t_new) * SCALE)
                top[half, g] = t_new
                total[half, g] = jnp.sum(w, axis=0, keepdims=True)
                acc[half, g] = jnp.dot(values_t, w.astype(jnp.bfloat16), preferred_element_type=jnp.float32)
        keys = kv[0, row_me, 0]
        values_t = jnp.transpose(kv[1, row_me, 0])
        visible = mask(segc[row_me, 0], seg_line(1))
        for g in range(HQ):
            top[1, g], total[1, g], acc[1, g] = update(g, 1, 1, keys, values_t, visible)

    def attend(row):
        keys = kv[0, row, 0]
        values_t = jnp.transpose(kv[1, row, 0])
        col = segc[row, 0]
        visible = mask(col, seg_line(1))
        for g in range(HQ):
            top[1, g], total[1, g], acc[1, g] = update(g, 1, 1, keys, values_t, visible)
        which = (pos_ref[row, 0] > pos_ref[row_me, 0]).astype(jnp.int32)
        late = which == 1
        keys = jnp.where(late, kv[0, row, 1], keys)
        values_t = jnp.transpose(jnp.where(late, kv[1, row, 1], kv[1, row, 0]))
        visible = mask(jnp.where(late, segc[row, 1], col), jnp.where(late, seg_line(1), seg_line(0)))
        for g in range(HQ):
            new = update(g, which, which, keys, values_t, visible)
            for ref, value in zip((top, total, acc), new):
                ref[0, g] = jnp.where(late, ref[0, g], value)
                ref[1, g] = jnp.where(late, value, ref[1, g])

    for r in range(Y):
        wait_row(z * Y + r)
        pass_on(z * Y + r)
    pltpu.make_async_copy(qbuf, qbuf, q_recv).wait()
    for r in range(Y):
        wait_sibling(z * Y + r)
    own()
    for r in range(1, Y):
        attend(z * Y + (t + r) % Y)

    def step(u, c):
        s, r = 1 + u // Y, u % Y

        def side(way, do):
            j = z + s * (2 * way - 1)

            @pl.when(jnp.logical_and(j >= 0, j < Z))
            def _():
                do(j * Y + r)

        def arrive(row):
            wait_row(row)
            pass_on(row)

        def use(row):
            wait_sibling(row)
            attend(row)

        def each(way, c):
            side(way, use)
            return c

        side(0, arrive)
        side(1, arrive)
        lax.fori_loop(0, 2, each, 0)
        return c

    lax.fori_loop(0, (Z - 1) * Y, step, 0)

    slot = kv_head * (2 // Y) + (t if Y == 1 else 0)
    out_cols = pl.ds(pl.multiple_of(slot * width, width), width)

    def send_out(half, wait):
        for e in range(HH):
            e = (e + 1) % HH
            i = half * HH + (h + e) % HH
            i_half, i_rows = part(i)
            send(obuf.at[i_half, i_rows, :], out_ref.at[:, out_cols],
                 out_send.at[half, e], out_recv, i, row_me, True, wait)

    for half in range(2):
        for g in range(HQ):
            o = acc[half, g] / total[half, g]
            obuf[half, :, g * HEAD_SIZE:(g + 1) * HEAD_SIZE] = jnp.transpose(o).astype(jnp.bfloat16)
        send_out(half, False)

    exchange(True)

    def drain(row, c):
        pass_on(row, True)
        return c

    lax.fori_loop(0, B, drain, 0)
    for half in range(2):
        send_out(half, True)
    pltpu.make_async_copy(out_ref, out_ref, out_recv).wait()


def local(queries, keys, values, position, segment):
    H, B = lax.axis_size("head"), lax.axis_size("blk")
    T = queries.shape[1]
    Y = 2 * KV_HEADS // H
    HQ = QUERY_HEADS // H
    R = position.shape[1] // 2
    pairs = B * (2 * R) ** 2 * HQ * 17 // 32
    out = pl.pallas_call(
        functools.partial(kernel, H, B),
        out_shape=jax.ShapeDtypeStruct((T, QUERY_HEADS * HEAD_SIZE), jnp.bfloat16),
        in_specs=[pl.BlockSpec(memory_space=pl.ANY)] * 3
        + [pl.BlockSpec(memory_space=pltpu.SMEM), pl.BlockSpec(memory_space=pltpu.VMEM)],
        out_specs=pl.BlockSpec(memory_space=pltpu.VMEM),
        scratch_shapes=[
            pltpu.VMEM((2, R, HQ * HEAD_SIZE), jnp.bfloat16),
            pltpu.VMEM((2, B, 2, R, HEAD_SIZE), jnp.bfloat16),
            pltpu.VMEM((B, 2, R, HEAD_SIZE), jnp.float32),
            pltpu.VMEM((2, R, HQ * HEAD_SIZE), jnp.bfloat16),
            pltpu.VMEM((2, HQ, 1, R), jnp.float32),
            pltpu.VMEM((2, HQ, 1, R), jnp.float32),
            pltpu.VMEM((2, HQ, HEAD_SIZE, R), jnp.float32),
            pltpu.SemaphoreType.DMA((2 + 2 // Y, KV_HEADS)),
            pltpu.SemaphoreType.DMA,
            pltpu.SemaphoreType.DMA((B,)),
            pltpu.SemaphoreType.DMA((B,)),
            pltpu.SemaphoreType.DMA((2, B)),
            pltpu.SemaphoreType.DMA((B,)),
            pltpu.SemaphoreType.DMA((2, H // 2)),
            pltpu.SemaphoreType.DMA,
        ],
        compiler_params=pltpu.CompilerParams(
            collective_id=0, has_side_effects=True, vmem_limit_bytes=40 * 2**20
        ),
        cost_estimate=pl.CostEstimate(
            flops=4 * pairs * HEAD_SIZE, bytes_accessed=8 * T * QUERY_HEADS * HEAD_SIZE, transcendentals=pairs
        ),
    )(queries[0], keys[0], values[0], position, segment)
    return out[None]


def solution(mesh):
    return jax.shard_map(
        local,
        mesh=mesh,
        in_specs=(P("blk", "head", None), P("blk", "head", None), P("blk", "head", None), P(), P()),
        out_specs=P("blk", "head", None),
        check_vma=False,
    )
```

time: 200 us -> 59.5 us (0.30)
  matrix products: 61.8 us -> 0 us
  Pallas kernels: 0 us -> 54.1 us
  waiting for transfers between devices: 53.2 us -> 0 us
  other arithmetic: 28.9 us -> 0 us
  blocking collectives: 27.1 us -> 0 us
  between operations: 13.7 us -> 0.01 us
  local copies, waits for them, and re-layouts: 10.8 us -> 5.08 us
  starting transfers between devices: 3.7 us -> 0 us
    dot_general x16 -> x0, matrix products: 61.8 us -> none  [the longest x8 32.2 us: absorb(): jnp.einsum('rkgc,ckd->rkgd', weights.astype(jnp.bfloat16), value_heads, p...]
    pallas_call x0 -> x1, Pallas kernels: none -> 54.1 us  [local(): pl.pallas_call(functools.partial(kernel, H, B), out_shape=jax.ShapeDtypeS...]
    all_gather x2 -> x0, waiting for transfers between devices: 44.7 us -> none  [the longest x1 41.1 us: local(): value_piece = lax.all_gather(value_heads, 'blk', axis=0, tiled=True)]
    all_to_all x3 -> x0, blocking collectives: 27.1 us -> none  [the longest x1 11.4 us: local(): lax.all_to_all(attended_local, 'head', split_axis=1, concat_axis=2, tiled...]
    unnamed x7 -> x0, other arithmetic: 17.9 us -> none
    all_to_all x1 -> x0, waiting for transfers between devices: 8.39 us -> none  [local(): lax.all_to_all(queries, 'head', split_axis=2, concat_axis=1, tiled=True)]
    reduce_sum x8 -> x0, other arithmetic: 8.38 us -> none  [absorb(): total_new = total_old * fade + jnp.sum(weights, axis=-1)]
    all_to_all x1 -> x0, starting transfers between devices: 3.65 us -> none  [local(): lax.all_to_all(queries, 'head', split_axis=2, concat_axis=1, tiled=True)]
  transfers between devices with their start and end apart: 3 -> 0, of which waited for: 3 -> 0; matrix products, arithmetic and copies ran while one was open for 9% -> 0% of each run, Pallas kernels for 0% -> 0%
where the time goes in v1:
time: 59.5 us; the launch traced here: 59.2 us
  Pallas kernels  54.1 us (91%)
  local copies, waits for them, and re-layouts  5.08 us (9%)
    pallas_call x1, Pallas kernels, local(): pl.pallas_call(functools.partial(kernel, H, B), out_shape=jax.ShapeDtypeS...  54.1 us
    unnamed x11, local copies, waits for them, and re-layouts  5.08 us

profile of v1, /device:TPU:0, one launch (start us, length us, event | category | flops | bytes accessed | tf_op | source)
XLA Modules:
  0.0 59.2 jit_solution(2185565815393919700)
XLA Ops:
  0.0 0.0 copy-start
  0.0 1.0 %copy-done = bf16[1,128,2048]{2,1,0:T(8,128)(2,1)S(1)} copy-done((bf16[1,128,2048]{2,1,0:T(8,128)(2,1)S(1)}, bf16[1,128,2048]{2,1,0:T(8,128)(2,1)}, u32[]{:S(2)}) %copy-start) | copy-done | bytes 524312
  1.0 0.0 copy-start.1
  1.0 0.9 %copy-done.1 = bf16[1,128,512]{2,1,0:T(8,128)(2,1)S(1)} copy-done((bf16[1,128,512]{2,1,0:T(8,128)(2,1)S(1)}, bf16[1,128,512]{2,1,0:T(8,128)(2,1)}, u32[]{:S(2)}) %copy-start.1) | copy-done | bytes 131096
  1.9 0.0 copy-start.2
  1.9 0.9 %copy-done.2 = bf16[1,128,512]{2,1,0:T(8,128)(2,1)S(1)} copy-done((bf16[1,128,512]{2,1,0:T(8,128)(2,1)S(1)}, bf16[1,128,512]{2,1,0:T(8,128)(2,1)}, u32[]{:S(2)}) %copy-start.2) | copy-done | bytes 131096
  2.9 0.0 copy-start.3
  2.9 0.7 %copy-done.3 = s32[8,512]{1,0:T(8,128)S(1)} copy-done((s32[8,512]{1,0:T(8,128)S(1)}, s32[8,512]{1,0:T(8,128)}, u32[]{:S(2)}) %copy-start.3) | copy-done | bytes 16408
  3.6 0.0 copy-start.4
  3.6 0.7 %copy-done.4 = s32[8,512]{1,0:T(8,128)S(1)} copy-done((s32[8,512]{1,0:T(8,128)S(1)}, s32[8,512]{1,0:T(8,128)}, u32[]{:S(2)}) %copy-start.4) | copy-done | bytes 16408
  4.3 54.1 %shard_map.55 = bf16[128,2048]{1,0:T(8,128)(2,1)S(1)} custom-call(bf16[128,2048]{1,0:T(8,128)(2,1)S(1)} %bitcast.5, bf16[128,512]{1,0:T(8,128)(2,1)S(1)} %bitcast.6, bf16[128,512]{1,0:T(8,128)(2,1)S(1)} %bitcast.7, s32[8,512]{1,0:T(8,128)S(1)} %copy-done.3, s32[8,512]{1,0:T(8,128)S(1)} %copy-done.4), custom_call_target="tpu_custom_call" | custom-call | flops 2281701376 | bytes 2097152 | tf_op jit(solution)/shard_map/pallas_call | solution.py:265
  58.4 0.8 %copy.7 = bf16[1,128,2048]{2,1,0:T(8,128)(2,1)} copy(bf16[1,128,2048]{2,1,0:T(8,128)(2,1)S(1)} %bitcast.4) | data formatting | bytes 1048576
Async XLA Ops:
  0.0 1.0 %copy-start = (bf16[1,128,2048]{2,1,0:T(8,128)(2,1)S(1)}, bf16[1,128,2048]{2,1,0:T(8,128)(2,1)}, u32[]{:S(2)}) copy-start(bf16[1,128,2048]{2,1,0:T(8,128)(2,1)} %param.5) | copy-start | bytes 1572868
  1.0 0.9 %copy-start.1 = (bf16[1,128,512]{2,1,0:T(8,128)(2,1)S(1)}, bf16[1,128,512]{2,1,0:T(8,128)(2,1)}, u32[]{:S(2)}) copy-start(bf16[1,128,512]{2,1,0:T(8,128)(2,1)} %param.6) | copy-start | bytes 393220
  1.9 0.9 %copy-start.2 = (bf16[1,128,512]{2,1,0:T(8,128)(2,1)S(1)}, bf16[1,128,512]{2,1,0:T(8,128)(2,1)}, u32[]{:S(2)}) copy-start(bf16[1,128,512]{2,1,0:T(8,128)(2,1)} %param.7) | copy-start | bytes 393220
  2.9 0.7 %copy-start.3 = (s32[8,512]{1,0:T(8,128)S(1)}, s32[8,512]{1,0:T(8,128)}, u32[]{:S(2)}) copy-start(s32[8,512]{1,0:T(8,128)} %pos_ref.1) | copy-start | bytes 49156
  3.6 0.7 %copy-start.4 = (s32[8,512]{1,0:T(8,128)S(1)}, s32[8,512]{1,0:T(8,128)}, u32[]{:S(2)}) copy-start(s32[8,512]{1,0:T(8,128)} %seg_ref.1) | copy-start | bytes 49156

commit v2 on v1

--- a/solution.py
+++ b/solution.py
@@ -17,7 +17,7 @@
 
 
 def kernel(H, B, q_in, k_in, v_in, pos_ref, seg_ref, out_ref,
-           qbuf, kv, segc, obuf, top, total, acc,
+           qbuf, kv, segc, obuf, top, total, acc, bias, pos_buf, seg_buf, small,
            first_send, q_recv, row_recv, sib_recv, fwd_send, sib_send, out_send, out_recv):
     Y = 2 * KV_HEADS // H
     Z = B // Y
@@ -33,6 +33,10 @@
     kv_head = chip * Y + y
     sibling = chip * 2 + 1 - t
     row_me = z * Y + t % Y
+
+    fetch = [pltpu.make_async_copy(pos_ref, pos_buf, small.at[0]), pltpu.make_async_copy(seg_ref, seg_buf, small.at[1])]
+    for copy in fetch:
+        copy.start()
 
     barrier = pltpu.get_barrier_semaphore()
     for i in range(H):
@@ -94,9 +98,11 @@
                      (k // Y) * 2 + core, z * Y + k % Y, d == 0, wait)
 
     exchange(False)
+    for copy in fetch:
+        copy.wait()
 
     def column(row, c):
-        line = seg_ref[pl.ds(row, 1), :].astype(jnp.float32)
+        line = seg_buf[pl.ds(row, 1), :].astype(jnp.float32)
         segc[row] = jnp.transpose(jnp.broadcast_to(line, (HEAD_SIZE, 2 * R))).reshape(2, R, HEAD_SIZE)
         return c
 
@@ -127,65 +133,64 @@
 
         copy(sibling, b, sib_send.at[row], sib_recv.at[row])
 
-    def scores(g, q_half, keys, visible):
+    def seg_line(q_half):
+        line = seg_buf[pl.ds(row_me, 1), :].astype(jnp.float32)
+        return line[:, q_half * R:(q_half + 1) * R]
+
+    def hide(n, col, line, extra=None):
+        visible = jnp.concatenate([col] * (R // HEAD_SIZE), axis=1) == line
+        if extra is not None:
+            visible = jnp.logical_and(visible, extra)
+        bias[n] = jnp.where(visible, 0.0, MASKED)
+
+    def tile(g, n, q_half, keys, values_t):
         q = qbuf[q_half, :, g * HEAD_SIZE:(g + 1) * HEAD_SIZE]
         s = lax.dot_general(keys, q, (((1,), (1,)), ((), ())), preferred_element_type=jnp.float32)
-        return jnp.where(visible, s, MASKED)
-
-    def seg_line(q_half):
-        line = seg_ref[pl.ds(row_me, 1), :].astype(jnp.float32)
-        return line[:, q_half * R:(q_half + 1) * R]
-
-    def mask(col, line):
-        return jnp.concatenate([col] * (R // HEAD_SIZE), axis=1) == line
-
-    def update(g, which, q_half, keys, values_t, visible):
-        s = scores(g, q_half, keys, visible)
-        top_old = top[which, g]
-        top_new = jnp.maximum(top_old, jnp.max(s, axis=0, keepdims=True))
-        w = jnp.exp2((s - top_new) * SCALE)
-        fade = jnp.exp2((top_old - top_new) * SCALE)
-        tot = total[which, g] * fade + jnp.sum(w, axis=0, keepdims=True)
-        a = acc[which, g] * fade + jnp.dot(values_t, w.astype(jnp.bfloat16), preferred_element_type=jnp.float32)
-        return top_new, tot, a
+        s = s + bias[n]
+        m = jnp.max(s, axis=0, keepdims=True)
+        w = jnp.exp2((s - m) * SCALE)
+        return (m, jnp.sum(w, axis=0, keepdims=True),
+                jnp.dot(values_t, w.astype(jnp.bfloat16), preferred_element_type=jnp.float32))
+
+    def merge(*states):
+        m = functools.reduce(jnp.maximum, [x[0] for x in states])
+        fades = [jnp.exp2((x[0] - m) * SCALE) for x in states]
+        return (m, sum(x[1] * f for x, f in zip(states, fades)),
+                sum(x[2] * f for x, f in zip(states, fades)))
+
+    def load(which, g):
+        return top[which, g], total[which, g], acc[which, g]
+
+    def store(which, g, state):
+        top[which, g], total[which, g], acc[which, g] = state
 
     def own():
         rows = lax.broadcasted_iota(jnp.int32, (R, R), 0)
         columns = lax.broadcasted_iota(jnp.int32, (R, R), 1)
+        keys = [kv[0, row_me, half] for half in range(2)]
+        values_t = [jnp.transpose(kv[1, row_me, half]) for half in range(2)]
         for half in range(2):
-            keys = kv[0, row_me, half]
-            values_t = jnp.transpose(kv[1, row_me, half])
-            visible = jnp.logical_and(mask(segc[row_me, half], seg_line(half)), rows <= columns)
-            for g in range(HQ):
-                s = scores(g, half, keys, visible)
-                t_new = jnp.max(s, axis=0, keepdims=True)
-                w = jnp.exp2((s - t_new) * SCALE)
-                top[half, g] = t_new
-                total[half, g] = jnp.sum(w, axis=0, keepdims=True)
-                acc[half, g] = jnp.dot(values_t, w.astype(jnp.bfloat16), preferred_element_type=jnp.float32)
-        keys = kv[0, row_me, 0]
-        values_t = jnp.transpose(kv[1, row_me, 0])
-        visible = mask(segc[row_me, 0], seg_line(1))
+            hide(half, segc[row_me, half], seg_line(half), rows <= columns)
+        hide(2, segc[row_me, 0], seg_line(1))
         for g in range(HQ):
-            top[1, g], total[1, g], acc[1, g] = update(g, 1, 1, keys, values_t, visible)
+            store(0, g, tile(g, 0, 0, keys[0], values_t[0]))
+            store(1, g, merge(tile(g, 1, 1, keys[1], values_t[1]), tile(g, 2, 1, keys[0], values_t[0])))
 
     def attend(row):
+        which = (pos_buf[row, 0] > pos_buf[row_me, 0]).astype(jnp.int32)
+        late = which == 1
         keys = kv[0, row, 0]
         values_t = jnp.transpose(kv[1, row, 0])
         col = segc[row, 0]
-        visible = mask(col, seg_line(1))
+        hide(0, col, seg_line(1))
+        keys_b = jnp.where(late, kv[0, row, 1], keys)
+        values_b = jnp.transpose(jnp.where(late, kv[1, row, 1], kv[1, row, 0]))
+        hide(1, jnp.where(late, segc[row, 1], col), jnp.where(late, seg_line(1), seg_line(0)))
         for g in range(HQ):
-            top[1, g], total[1, g], acc[1, g] = update(g, 1, 1, keys, values_t, visible)
-        which = (pos_ref[row, 0] > pos_ref[row_me, 0]).astype(jnp.int32)
-        late = which == 1
-        keys = jnp.where(late, kv[0, row, 1], keys)
-        values_t = jnp.transpose(jnp.where(late, kv[1, row, 1], kv[1, row, 0]))
-        visible = mask(jnp.where(late, segc[row, 1], col), jnp.where(late, seg_line(1), seg_line(0)))
-        for g in range(HQ):
-            new = update(g, which, which, keys, values_t, visible)
-            for ref, value in zip((top, total, acc), new):
-                ref[0, g] = jnp.where(late, ref[0, g], value)
-                ref[1, g] = jnp.where(late, value, ref[1, g])
+            one = tile(g, 0, 1, keys, values_t)
+            m, tot, a = tile(g, 1, which, keys_b, values_b)
+            store(1, g, merge(load(1, g), one, (jnp.where(late, m, MASKED), tot, a)))
+            store(0, g, merge(load(0, g), (jnp.where(late, MASKED, m), tot, a)))
 
     for r in range(Y):
         wait_row(z * Y + r)
@@ -265,9 +270,8 @@
     out = pl.pallas_call(
         functools.partial(kernel, H, B),
         out_shape=jax.ShapeDtypeStruct((T, QUERY_HEADS * HEAD_SIZE), jnp.bfloat16),
-        in_specs=[pl.BlockSpec(memory_space=pl.ANY)] * 3
-        + [pl.BlockSpec(memory_space=pltpu.SMEM), pl.BlockSpec(memory_space=pltpu.VMEM)],
-        out_specs=pl.BlockSpec(memory_space=pltpu.VMEM),
+        in_specs=[pl.BlockSpec(memory_space=pltpu.HBM)] * 5,
+        out_specs=pl.BlockSpec(memory_space=pl.ANY),
         scratch_shapes=[
             pltpu.VMEM((2, R, HQ * HEAD_SIZE), jnp.bfloat16),
             pltpu.VMEM((2, B, 2, R, HEAD_SIZE), jnp.bfloat16),
@@ -276,6 +280,10 @@
             pltpu.VMEM((2, HQ, 1, R), jnp.float32),
             pltpu.VMEM((2, HQ, 1, R), jnp.float32),
             pltpu.VMEM((2, HQ, HEAD_SIZE, R), jnp.float32),
+            pltpu.VMEM((3, R, R), jnp.float32),
+            pltpu.SMEM(position.shape, jnp.int32),
+            pltpu.VMEM(segment.shape, jnp.int32),
+            pltpu.SemaphoreType.DMA((2,)),
             pltpu.SemaphoreType.DMA((2 + 2 // Y, KV_HEADS)),
             pltpu.SemaphoreType.DMA,
             pltpu.SemaphoreType.DMA((B,)),
@@ -286,7 +294,7 @@
             pltpu.SemaphoreType.DMA,
         ],
         compiler_params=pltpu.CompilerParams(
-            collective_id=0, has_side_effects=True, vmem_limit_bytes=40 * 2**20
+            collective_id=0, has_side_effects=True, vmem_limit_bytes=60 * 2**20
         ),
         cost_estimate=pl.CostEstimate(
             flops=4 * pairs * HEAD_SIZE, bytes_accessed=8 * T * QUERY_HEADS * HEAD_SIZE, transcendentals=pairs

time: 59.5 us -> 56.2 us (0.945)
  local copies, waits for them, and re-layouts: 5.08 us -> 1.88 us
    unnamed x11 -> x1, local copies, waits for them, and re-layouts: 5.08 us -> 1.88 us
where the time goes in v2:
time: 56.2 us; the launch traced here: 56 us
  Pallas kernels  54.1 us (96%)
  local copies, waits for them, and re-layouts  1.88 us (3%)
    pallas_call x1, Pallas kernels, local(): pl.pallas_call(functools.partial(kernel, H, B), out_shape=jax.ShapeDtypeS...  54.1 us
    unnamed x1, local copies, waits for them, and re-layouts  1.88 us

profile of v2, /device:TPU:0, one launch (start us, length us, event | category | flops | bytes accessed | tf_op | source)
XLA Modules:
  0.0 56.0 jit_solution(4451245091751859958)
XLA Ops:
  0.0 54.1 %shard_map.55 = bf16[128,2048]{1,0:T(8,128)(2,1)} custom-call(bf16[128,2048]{1,0:T(8,128)(2,1)} %bitcast.5, bf16[128,512]{1,0:T(8,128)(2,1)} %bitcast.6, bf16[128,512]{1,0:T(8,128)(2,1)} %bitcast.7, s32[8,512]{1,0:T(8,128)} %pos_ref.1, s32[8,512]{1,0:T(8,128)} %seg_ref.1), custom_call_target="tpu_custom_call" | custom-call | flops 2281701376 | bytes 2097152 | tf_op jit(solution)/shard_map/pallas_call | solution.py:270
  54.1 1.9 %copy.7 = bf16[1,128,2048]{2,1,0:T(8,128)(2,1)} copy(bf16[1,128,2048]{2,1,0:T(8,128)(2,1)} %bitcast.4) | data formatting | bytes 1048576

commit v3 on v2

--- a/solution.py
+++ b/solution.py
@@ -78,7 +78,7 @@
             def _():
                 pltpu.make_async_copy(src, dst, recv_sem).start()
 
-    def exchange(wait):
+    def exchange_kv(wait):
         for n, array in enumerate((k_in, v_in)):
             for d in range(KV_HEADS):
                 d = (d + 1) % KV_HEADS
@@ -87,6 +87,8 @@
                 send(array.at[:, cols], kv.at[n, b, my_half, my_rows, :],
                      first_send.at[n, d], row_recv.at[b],
                      (k // Y) * 2 + n, z * Y + k % Y, d == 0, wait)
+
+    def exchange_q(wait):
         for half in range(2 // Y):
             for d in range(KV_HEADS):
                 d = (d + 1) % KV_HEADS
@@ -96,17 +98,6 @@
                 send(q_in.at[:, cols], qbuf.at[my_half, my_rows, :],
                      first_send.at[2 + half, d], q_recv,
                      (k // Y) * 2 + core, z * Y + k % Y, d == 0, wait)
-
-    exchange(False)
-    for copy in fetch:
-        copy.wait()
-
-    def column(row, c):
-        line = seg_buf[pl.ds(row, 1), :].astype(jnp.float32)
-        segc[row] = jnp.transpose(jnp.broadcast_to(line, (HEAD_SIZE, 2 * R))).reshape(2, R, HEAD_SIZE)
-        return c
-
-    lax.fori_loop(0, B, column, 0)
 
     def wait_row(row):
         pltpu.make_async_copy(kv.at[t, row], kv.at[t, row], row_recv.at[row]).wait()
@@ -192,44 +183,74 @@
             store(1, g, merge(load(1, g), one, (jnp.where(late, m, MASKED), tot, a)))
             store(0, g, merge(load(0, g), (jnp.where(late, MASKED, m), tot, a)))
 
+    def side(u, way, do):
+        j = z + (1 + u // Y) * (2 * way - 1)
+
+        @pl.when(jnp.logical_and(j >= 0, j < Z))
+        def _():
+            do(j * Y + u % Y)
+
+    def arrive_row(row):
+        wait_row(row)
+        pass_on(row)
+
+    def use_row(row):
+        wait_sibling(row)
+        attend(row)
+
+    def arrive(u):
+        side(u, 0, arrive_row)
+        side(u, 1, arrive_row)
+
+    exchange_kv(False)
+    for copy in fetch:
+        copy.wait()
     for r in range(Y):
         wait_row(z * Y + r)
         pass_on(z * Y + r)
+    exchange_q(False)
+
+    def column(row, c):
+        line = seg_buf[pl.ds(row, 1), :].astype(jnp.float32)
+        segc[row] = jnp.transpose(jnp.broadcast_to(line, (HEAD_SIZE, 2 * R))).reshape(2, R, HEAD_SIZE)
+        return c
+
+    lax.fori_loop(0, B, column, 0)
+
+    units = (Z - 1) * Y
+    between = jnp.logical_and(z > 0, z < Z - 1)
+    ahead = jnp.where(between, 4, 2)
+    for u in range(min(2, units)):
+        arrive(u)
     pltpu.make_async_copy(qbuf, qbuf, q_recv).wait()
     for r in range(Y):
         wait_sibling(z * Y + r)
     own()
+
+    def early(u):
+        @pl.when(jnp.logical_and(between, u < units))
+        def _():
+            arrive(u)
+
+    early(2)
     for r in range(1, Y):
         attend(z * Y + (t + r) % Y)
+    early(3)
 
     def step(u, c):
-        s, r = 1 + u // Y, u % Y
-
-        def side(way, do):
-            j = z + s * (2 * way - 1)
-
-            @pl.when(jnp.logical_and(j >= 0, j < Z))
-            def _():
-                do(j * Y + r)
-
-        def arrive(row):
-            wait_row(row)
-            pass_on(row)
-
-        def use(row):
-            wait_sibling(row)
-            attend(row)
-
         def each(way, c):
-            side(way, use)
+            side(u, way, use_row)
             return c
 
-        side(0, arrive)
-        side(1, arrive)
         lax.fori_loop(0, 2, each, 0)
+
+        @pl.when(u + ahead < units)
+        def _():
+            arrive(u + ahead)
+
         return c
 
-    lax.fori_loop(0, (Z - 1) * Y, step, 0)
+    lax.fori_loop(0, units, step, 0)
 
     slot = kv_head * (2 // Y) + (t if Y == 1 else 0)
     out_cols = pl.ds(pl.multiple_of(slot * width, width), width)
@@ -248,7 +269,8 @@
             obuf[half, :, g * HEAD_SIZE:(g + 1) * HEAD_SIZE] = jnp.transpose(o).astype(jnp.bfloat16)
         send_out(half, False)
 
-    exchange(True)
+    exchange_kv(True)
+    exchange_q(True)
 
     def drain(row, c):
         pass_on(row, True)

time: 56.2 us -> 49.7 us (0.88)
  Pallas kernels: 54.1 us -> 47.6 us
    pallas_call x1, Pallas kernels: 54.1 us -> 47.6 us  [local(): pl.pallas_call(functools.partial(kernel, H, B), out_shape=jax.ShapeDtypeS...]
where the time goes in v3:
time: 49.7 us; the launch traced here: 49.5 us
  Pallas kernels  47.6 us (96%)
  local copies, waits for them, and re-layouts  1.88 us (4%)
    pallas_call x1, Pallas kernels, local(): pl.pallas_call(functools.partial(kernel, H, B), out_shape=jax.ShapeDtypeS...  47.6 us
    unnamed x1, local copies, waits for them, and re-layouts  1.88 us

profile of v3, /device:TPU:0, one launch (start us, length us, event | category | flops | bytes accessed | tf_op | source)
XLA Modules:
  0.0 49.5 jit_solution(11629890093894327354)
XLA Ops:
  0.0 47.6 %shard_map.55 = bf16[128,2048]{1,0:T(8,128)(2,1)} custom-call(bf16[128,2048]{1,0:T(8,128)(2,1)} %bitcast.5, bf16[128,512]{1,0:T(8,128)(2,1)} %bitcast.6, bf16[128,512]{1,0:T(8,128)(2,1)} %bitcast.7, s32[8,512]{1,0:T(8,128)} %pos_ref.1, s32[8,512]{1,0:T(8,128)} %seg_ref.1), custom_call_target="tpu_custom_call" | custom-call | flops 2281701376 | bytes 2097152 | tf_op jit(solution)/shard_map/pallas_call | solution.py:292
  47.7 1.9 %copy.7 = bf16[1,128,2048]{2,1,0:T(8,128)(2,1)} copy(bf16[1,128,2048]{2,1,0:T(8,128)(2,1)} %bitcast.4) | data formatting | bytes 1048576

commit v4 on v3

--- a/solution.py
+++ b/solution.py
@@ -17,7 +17,7 @@
 
 
 def kernel(H, B, q_in, k_in, v_in, pos_ref, seg_ref, out_ref,
-           qbuf, kv, segc, obuf, top, total, acc, bias, pos_buf, seg_buf, small,
+           qbuf, kv, segc, obuf, top, total, acc, qt, pos_buf, seg_buf, small,
            first_send, q_recv, row_recv, sib_recv, fwd_send, sib_send, out_send, out_recv):
     Y = 2 * KV_HEADS // H
     Z = B // Y
@@ -128,16 +128,18 @@
         line = seg_buf[pl.ds(row_me, 1), :].astype(jnp.float32)
         return line[:, q_half * R:(q_half + 1) * R]
 
-    def hide(n, col, line, extra=None):
+    def hide(col, line, extra=None):
         visible = jnp.concatenate([col] * (R // HEAD_SIZE), axis=1) == line
         if extra is not None:
             visible = jnp.logical_and(visible, extra)
-        bias[n] = jnp.where(visible, 0.0, MASKED)
-
-    def tile(g, n, q_half, keys, values_t):
-        q = qbuf[q_half, :, g * HEAD_SIZE:(g + 1) * HEAD_SIZE]
-        s = lax.dot_general(keys, q, (((1,), (1,)), ((), ())), preferred_element_type=jnp.float32)
-        s = s + bias[n]
+        bias = jnp.where(visible, 0.0, MASKED)
+        return jnp.concatenate([bias] * HQ, axis=1)
+
+    def scores(keys, q_half):
+        return jnp.dot(keys, qt[q_half], preferred_element_type=jnp.float32)
+
+    def tile(s, bias, values_t):
+        s = s + bias
         m = jnp.max(s, axis=0, keepdims=True)
         w = jnp.exp2((s - m) * SCALE)
         return (m, jnp.sum(w, axis=0, keepdims=True),
@@ -149,11 +151,11 @@
         return (m, sum(x[1] * f for x, f in zip(states, fades)),
                 sum(x[2] * f for x, f in zip(states, fades)))
 
-    def load(which, g):
-        return top[which, g], total[which, g], acc[which, g]
-
-    def store(which, g, state):
-        top[which, g], total[which, g], acc[which, g] = state
+    def load(which):
+        return top[which], total[which], acc[which]
+
+    def store(which, state):
+        top[which], total[which], acc[which] = state
 
     def own():
         rows = lax.broadcasted_iota(jnp.int32, (R, R), 0)
@@ -161,27 +163,31 @@
         keys = [kv[0, row_me, half] for half in range(2)]
         values_t = [jnp.transpose(kv[1, row_me, half]) for half in range(2)]
         for half in range(2):
-            hide(half, segc[row_me, half], seg_line(half), rows <= columns)
-        hide(2, segc[row_me, 0], seg_line(1))
-        for g in range(HQ):
-            store(0, g, tile(g, 0, 0, keys[0], values_t[0]))
-            store(1, g, merge(tile(g, 1, 1, keys[1], values_t[1]), tile(g, 2, 1, keys[0], values_t[0])))
+            for g in range(HQ):
+                qt[half, :, g * R:(g + 1) * R] = jnp.transpose(qbuf[half, :, g * HEAD_SIZE:(g + 1) * HEAD_SIZE])
+        s = [scores(keys[0], 0), scores(keys[1], 1), scores(keys[0], 1)]
+        first = tile(s[0], hide(segc[row_me, 0], seg_line(0), rows <= columns), values_t[0])
+        second = tile(s[1], hide(segc[row_me, 1], seg_line(1), rows <= columns), values_t[1])
+        third = tile(s[2], hide(segc[row_me, 0], seg_line(1)), values_t[0])
+        store(0, first)
+        store(1, merge(second, third))
 
     def attend(row):
         which = (pos_buf[row, 0] > pos_buf[row_me, 0]).astype(jnp.int32)
         late = which == 1
         keys = kv[0, row, 0]
-        values_t = jnp.transpose(kv[1, row, 0])
+        values = kv[1, row, 0]
         col = segc[row, 0]
-        hide(0, col, seg_line(1))
-        keys_b = jnp.where(late, kv[0, row, 1], keys)
-        values_b = jnp.transpose(jnp.where(late, kv[1, row, 1], kv[1, row, 0]))
-        hide(1, jnp.where(late, segc[row, 1], col), jnp.where(late, seg_line(1), seg_line(0)))
-        for g in range(HQ):
-            one = tile(g, 0, 1, keys, values_t)
-            m, tot, a = tile(g, 1, which, keys_b, values_b)
-            store(1, g, merge(load(1, g), one, (jnp.where(late, m, MASKED), tot, a)))
-            store(0, g, merge(load(0, g), (jnp.where(late, MASKED, m), tot, a)))
+        s_a = scores(keys, 1)
+        s_b = scores(jnp.where(late, kv[0, row, 1], keys), which)
+        one = tile(s_a, hide(col, seg_line(1)), jnp.transpose(values))
+        m, tot, a = tile(
+            s_b, hide(jnp.where(late, segc[row, 1], col), jnp.where(late, seg_line(1), seg_line(0))),
+            jnp.transpose(jnp.where(late, kv[1, row, 1], values)))
+        early = merge(load(0), (jnp.where(late, MASKED, m), tot, a))
+        later = merge(load(1), one, (jnp.where(late, m, MASKED), tot, a))
+        store(0, early)
+        store(1, later)
 
     def side(u, way, do):
         j = z + (1 + u // Y) * (2 * way - 1)
@@ -265,7 +271,7 @@
 
     for half in range(2):
         for g in range(HQ):
-            o = acc[half, g] / total[half, g]
+            o = acc[half, :, g * R:(g + 1) * R] / total[half, :, g * R:(g + 1) * R]
             obuf[half, :, g * HEAD_SIZE:(g + 1) * HEAD_SIZE] = jnp.transpose(o).astype(jnp.bfloat16)
         send_out(half, False)
 
@@ -299,10 +305,10 @@
             pltpu.VMEM((2, B, 2, R, HEAD_SIZE), jnp.bfloat16),
             pltpu.VMEM((B, 2, R, HEAD_SIZE), jnp.float32),
             pltpu.VMEM((2, R, HQ * HEAD_SIZE), jnp.bfloat16),
-            pltpu.VMEM((2, HQ, 1, R), jnp.float32),
-            pltpu.VMEM((2, HQ, 1, R), jnp.float32),
-            pltpu.VMEM((2, HQ, HEAD_SIZE, R), jnp.float32),
-            pltpu.VMEM((3, R, R), jnp.float32),
+            pltpu.VMEM((2, 1, HQ * R), jnp.float32),
+            pltpu.VMEM((2, 1, HQ * R), jnp.float32),
+            pltpu.VMEM((2, HEAD_SIZE, HQ * R), jnp.float32),
+            pltpu.VMEM((2, HEAD_SIZE, HQ * R), jnp.bfloat16),
             pltpu.SMEM(position.shape, jnp.int32),
             pltpu.VMEM(segment.shape, jnp.int32),
             pltpu.SemaphoreType.DMA((2,)),

time: 49.7 us -> 41.9 us (0.84)
  Pallas kernels: 47.6 us -> 39.8 us
    pallas_call x1, Pallas kernels: 47.6 us -> 39.8 us  [local(): pl.pallas_call(functools.partial(kernel, H, B), out_shape=jax.ShapeDtypeS...]
where the time goes in v4:
time: 41.9 us; the launch traced here: 41.7 us
  Pallas kernels  39.8 us (95%)
  local copies, waits for them, and re-layouts  1.88 us (4%)
    pallas_call x1, Pallas kernels, local(): pl.pallas_call(functools.partial(kernel, H, B), out_shape=jax.ShapeDtypeS...  39.8 us
    unnamed x1, local copies, waits for them, and re-layouts  1.88 us

profile of v4, /device:TPU:0, one launch (start us, length us, event | category | flops | bytes accessed | tf_op | source)
XLA Modules:
  0.0 41.7 jit_solution(11443317413074556752)
XLA Ops:
  0.0 39.8 %shard_map.55 = bf16[128,2048]{1,0:T(8,128)(2,1)} custom-call(bf16[128,2048]{1,0:T(8,128)(2,1)} %bitcast.5, bf16[128,512]{1,0:T(8,128)(2,1)} %bitcast.6, bf16[128,512]{1,0:T(8,128)(2,1)} %bitcast.7, s32[8,512]{1,0:T(8,128)} %pos_ref.1, s32[8,512]{1,0:T(8,128)} %seg_ref.1), custom_call_target="tpu_custom_call" | custom-call | flops 2281701376 | bytes 2097152 | tf_op jit(solution)/shard_map/pallas_call | solution.py:298
  39.8 1.9 %copy.7 = bf16[1,128,2048]{2,1,0:T(8,128)(2,1)} copy(bf16[1,128,2048]{2,1,0:T(8,128)(2,1)} %bitcast.4) | data formatting | bytes 1048576

commit v5 on v4

--- a/solution.py
+++ b/solution.py
@@ -172,22 +172,45 @@
         store(0, first)
         store(1, merge(second, third))
 
+    def choose(row):
+        which = (pos_buf[row, 0] > pos_buf[row_me, 0]).astype(jnp.int32)
+        return which, which == 1
+
+    def fixed_scores(row):
+        return scores(kv[0, row, 0], 1)
+
+    def fixed_tile(row, s):
+        return tile(s, hide(segc[row, 0], seg_line(1)), jnp.transpose(kv[1, row, 0]))
+
+    def other_scores(row):
+        which, late = choose(row)
+        return scores(jnp.where(late, kv[0, row, 1], kv[0, row, 0]), which)
+
+    def other_tile(row, s):
+        which, late = choose(row)
+        col = jnp.where(late, segc[row, 1], segc[row, 0])
+        m, tot, a = tile(s, hide(col, jnp.where(late, seg_line(1), seg_line(0))),
+                         jnp.transpose(jnp.where(late, kv[1, row, 1], kv[1, row, 0])))
+        return (jnp.where(late, MASKED, m), tot, a), (jnp.where(late, m, MASKED), tot, a)
+
     def attend(row):
-        which = (pos_buf[row, 0] > pos_buf[row_me, 0]).astype(jnp.int32)
-        late = which == 1
-        keys = kv[0, row, 0]
-        values = kv[1, row, 0]
-        col = segc[row, 0]
-        s_a = scores(keys, 1)
-        s_b = scores(jnp.where(late, kv[0, row, 1], keys), which)
-        one = tile(s_a, hide(col, seg_line(1)), jnp.transpose(values))
-        m, tot, a = tile(
-            s_b, hide(jnp.where(late, segc[row, 1], col), jnp.where(late, seg_line(1), seg_line(0))),
-            jnp.transpose(jnp.where(late, kv[1, row, 1], values)))
-        early = merge(load(0), (jnp.where(late, MASKED, m), tot, a))
-        later = merge(load(1), one, (jnp.where(late, m, MASKED), tot, a))
+        s_a, s_b = fixed_scores(row), other_scores(row)
+        one = fixed_tile(row, s_a)
+        to_early, to_later = other_tile(row, s_b)
+        early = merge(load(0), to_early)
+        later = merge(load(1), one, to_later)
         store(0, early)
         store(1, later)
+
+    def attend_other(row):
+        wait_sibling(row)
+        to_early, to_later = other_tile(row, other_scores(row))
+        early, later = merge(load(0), to_early), merge(load(1), to_later)
+        store(0, early)
+        store(1, later)
+
+    def attend_fixed(row):
+        store(1, merge(load(1), fixed_tile(row, fixed_scores(row))))
 
     def side(u, way, do):
         j = z + (1 + u // Y) * (2 * way - 1)
@@ -256,7 +279,17 @@
 
         return c
 
-    lax.fori_loop(0, units, step, 0)
+    last = jnp.maximum(z, Z - 1 - z) * Y - 1
+    lax.fori_loop(0, last, step, 0)
+
+    def each_side(do):
+        def each(way, c):
+            side(last, way, do)
+            return c
+
+        lax.fori_loop(0, 2, each, 0)
+
+    each_side(attend_other)
 
     slot = kv_head * (2 // Y) + (t if Y == 1 else 0)
     out_cols = pl.ds(pl.multiple_of(slot * width, width), width)
@@ -270,9 +303,12 @@
                  out_send.at[half, e], out_recv, i, row_me, True, wait)
 
     for half in range(2):
+        if half == 1:
+            each_side(attend_fixed)
+        outs = acc[half] * (1.0 / total[half])
         for g in range(HQ):
-            o = acc[half, :, g * R:(g + 1) * R] / total[half, :, g * R:(g + 1) * R]
-            obuf[half, :, g * HEAD_SIZE:(g + 1) * HEAD_SIZE] = jnp.transpose(o).astype(jnp.bfloat16)
+            o = jnp.transpose(outs[:, g * R:(g + 1) * R]).astype(jnp.bfloat16)
+            obuf[half, :, g * HEAD_SIZE:(g + 1) * HEAD_SIZE] = o
         send_out(half, False)
 
     exchange_kv(True)

time: 41.9 us -> 41.2 us (0.983)
  Pallas kernels: 39.8 us -> 39.2 us
    pallas_call x1, Pallas kernels: 39.8 us -> 39.2 us  [local(): pl.pallas_call(functools.partial(kernel, H, B), out_shape=jax.ShapeDtypeS...]
where the time goes in v5:
time: 41.2 us; the launch traced here: 41 us
  Pallas kernels  39.2 us (95%)
  local copies, waits for them, and re-layouts  1.88 us (5%)
    pallas_call x1, Pallas kernels, local(): pl.pallas_call(functools.partial(kernel, H, B), out_shape=jax.ShapeDtypeS...  39.2 us
    unnamed x1, local copies, waits for them, and re-layouts  1.88 us

profile of v5, /device:TPU:0, one launch (start us, length us, event | category | flops | bytes accessed | tf_op | source)
XLA Modules:
  0.0 41.0 jit_solution(1290161061388443791)
XLA Ops:
  0.0 39.2 %shard_map.55 = bf16[128,2048]{1,0:T(8,128)(2,1)} custom-call(bf16[128,2048]{1,0:T(8,128)(2,1)} %bitcast.5, bf16[128,512]{1,0:T(8,128)(2,1)} %bitcast.6, bf16[128,512]{1,0:T(8,128)(2,1)} %bitcast.7, s32[8,512]{1,0:T(8,128)} %pos_ref.1, s32[8,512]{1,0:T(8,128)} %seg_ref.1), custom_call_target="tpu_custom_call" | custom-call | flops 2281701376 | bytes 2097152 | tf_op jit(solution)/shard_map/pallas_call | solution.py:334
  39.2 1.9 %copy.7 = bf16[1,128,2048]{2,1,0:T(8,128)(2,1)} copy(bf16[1,128,2048]{2,1,0:T(8,128)(2,1)} %bitcast.4) | data formatting | bytes 1048576

commit v6 on v5

--- a/solution.py
+++ b/solution.py
@@ -232,12 +232,12 @@
         side(u, 1, arrive_row)
 
     exchange_kv(False)
+    exchange_q(False)
     for copy in fetch:
         copy.wait()
     for r in range(Y):
         wait_row(z * Y + r)
         pass_on(z * Y + r)
-    exchange_q(False)
 
     def column(row, c):
         line = seg_buf[pl.ds(row, 1), :].astype(jnp.float32)
@@ -296,7 +296,6 @@
 
     def send_out(half, wait):
         for e in range(HH):
-            e = (e + 1) % HH
             i = half * HH + (h + e) % HH
             i_half, i_rows = part(i)
             send(obuf.at[i_half, i_rows, :], out_ref.at[:, out_cols],

time: 41.2 us -> 40.6 us (0.985)
  the two profiles are of different devices: /device:TPU:0 before, /device:TPU:1 now
where the time goes in v6:
time: 40.6 us; the launch traced here: 40.4 us
  Pallas kernels  38.5 us (95%)
  local copies, waits for them, and re-layouts  1.88 us (5%)
    pallas_call x1, Pallas kernels, local(): pl.pallas_call(functools.partial(kernel, H, B), out_shape=jax.ShapeDtypeS...  38.5 us
    unnamed x1, local copies, waits for them, and re-layouts  1.88 us

profile of v6, /device:TPU:1, one launch (start us, length us, event | category | flops | bytes accessed | tf_op | source)
XLA Modules:
  0.0 40.4 jit_solution(485276571120353683)
XLA Ops:
  0.0 38.5 %shard_map.55 = bf16[128,2048]{1,0:T(8,128)(2,1)} custom-call(bf16[128,2048]{1,0:T(8,128)(2,1)} %bitcast.5, bf16[128,512]{1,0:T(8,128)(2,1)} %bitcast.6, bf16[128,512]{1,0:T(8,128)(2,1)} %bitcast.7, s32[8,512]{1,0:T(8,128)} %pos_ref.1, s32[8,512]{1,0:T(8,128)} %seg_ref.1), custom_call_target="tpu_custom_call" | custom-call | flops 2281701376 | bytes 2097152 | tf_op jit(solution)/shard_map/pallas_call | solution.py:333
  38.6 1.9 %copy.7 = bf16[1,128,2048]{2,1,0:T(8,128)(2,1)} copy(bf16[1,128,2048]{2,1,0:T(8,128)(2,1)} %bitcast.4) | data formatting | bytes 1048576

commit v7 on v6

--- a/solution.py
+++ b/solution.py
@@ -215,7 +215,7 @@
     def side(u, way, do):
         j = z + (1 + u // Y) * (2 * way - 1)
 
-        @pl.when(jnp.logical_and(j >= 0, j < Z))
+        @pl.when(jnp.logical_and(jnp.logical_and(j >= 0, j < Z), u >= 0))
         def _():
             do(j * Y + u % Y)
 
@@ -280,16 +280,26 @@
         return c
 
     last = jnp.maximum(z, Z - 1 - z) * Y - 1
-    lax.fori_loop(0, last, step, 0)
-
-    def each_side(do):
-        def each(way, c):
-            side(last, way, do)
-            return c
-
-        lax.fori_loop(0, 2, each, 0)
-
-    each_side(attend_other)
+    held = 3
+    lax.fori_loop(0, jnp.maximum(last + 1 - held, 0), step, 0)
+
+    def tail(k, way, do):
+        side(last + 1 - held + k, way, do)
+
+    def other_tail(k, c):
+        lax.fori_loop(0, 2, lambda way, c: (tail(k, way, attend_other), c)[1], 0)
+
+        @pl.when(jnp.logical_and(k + 2 - held == -1, jnp.logical_not(between)))
+        def _():
+            arrive(last)
+
+        return c
+
+    def fixed_tail(k, c):
+        lax.fori_loop(0, 2, lambda way, c: (tail(k, way, attend_fixed), c)[1], 0)
+        return c
+
+    lax.fori_loop(0, held, other_tail, 0)
 
     slot = kv_head * (2 // Y) + (t if Y == 1 else 0)
     out_cols = pl.ds(pl.multiple_of(slot * width, width), width)
@@ -303,7 +313,7 @@
 
     for half in range(2):
         if half == 1:
-            each_side(attend_fixed)
+            lax.fori_loop(0, held, fixed_tail, 0)
         outs = acc[half] * (1.0 / total[half])
         for g in range(HQ):
             o = jnp.transpose(outs[:, g * R:(g + 1) * R]).astype(jnp.bfloat16)

time: 40.6 us -> 41.2 us (1.015)
  the two profiles are of different devices: /device:TPU:1 before, /device:TPU:3 now
where the time goes in v7:
time: 41.2 us; the launch traced here: 41 us
  Pallas kernels  39.1 us (95%)
  local copies, waits for them, and re-layouts  1.88 us (5%)
    pallas_call x1, Pallas kernels, local(): pl.pallas_call(functools.partial(kernel, H, B), out_shape=jax.ShapeDtypeS...  39.1 us
    unnamed x1, local copies, waits for them, and re-layouts  1.88 us

profile of v7, /device:TPU:3, one launch (start us, length us, event | category | flops | bytes accessed | tf_op | source)
XLA Modules:
  0.0 41.0 jit_solution(14268885496421904540)
XLA Ops:
  0.0 39.1 %shard_map.55 = bf16[128,2048]{1,0:T(8,128)(2,1)} custom-call(bf16[128,2048]{1,0:T(8,128)(2,1)} %bitcast.5, bf16[128,512]{1,0:T(8,128)(2,1)} %bitcast.6, bf16[128,512]{1,0:T(8,128)(2,1)} %bitcast.7, s32[8,512]{1,0:T(8,128)} %pos_ref.1, s32[8,512]{1,0:T(8,128)} %seg_ref.1), custom_call_target="tpu_custom_call" | custom-call | flops 2281701376 | bytes 2097152 | tf_op jit(solution)/shard_map/pallas_call | solution.py:343
  39.1 1.9 %copy.7 = bf16[1,128,2048]{2,1,0:T(8,128)(2,1)} copy(bf16[1,128,2048]{2,1,0:T(8,128)(2,1)} %bitcast.4) | data formatting | bytes 1048576

commit v8 on v7

--- a/solution.py
+++ b/solution.py
@@ -280,7 +280,7 @@
         return c
 
     last = jnp.maximum(z, Z - 1 - z) * Y - 1
-    held = 3
+    held = jnp.where(between, 3, 1)
     lax.fori_loop(0, jnp.maximum(last + 1 - held, 0), step, 0)
 
     def tail(k, way, do):

time: 41.2 us -> 40.6 us (0.985)
  the two profiles are of different devices: /device:TPU:3 before, /device:TPU:1 now
where the time goes in v8:
time: 40.6 us; the launch traced here: 40.5 us
  Pallas kernels  38.6 us (95%)
  local copies, waits for them, and re-layouts  1.88 us (5%)
    pallas_call x1, Pallas kernels, local(): pl.pallas_call(functools.partial(kernel, H, B), out_shape=jax.ShapeDtypeS...  38.6 us
    unnamed x1, local copies, waits for them, and re-layouts  1.88 us

profile of v8, /device:TPU:1, one launch (start us, length us, event | category | flops | bytes accessed | tf_op | source)
XLA Modules:
  0.0 40.5 jit_solution(5146256194372999899)
XLA Ops:
  0.0 38.6 %shard_map.55 = bf16[128,2048]{1,0:T(8,128)(2,1)} custom-call(bf16[128,2048]{1,0:T(8,128)(2,1)} %bitcast.5, bf16[128,512]{1,0:T(8,128)(2,1)} %bitcast.6, bf16[128,512]{1,0:T(8,128)(2,1)} %bitcast.7, s32[8,512]{1,0:T(8,128)} %pos_ref.1, s32[8,512]{1,0:T(8,128)} %seg_ref.1), custom_call_target="tpu_custom_call" | custom-call | flops 2281701376 | bytes 2097152 | tf_op jit(solution)/shard_map/pallas_call | solution.py:343
  38.6 1.9 %copy.7 = bf16[1,128,2048]{2,1,0:T(8,128)(2,1)} copy(bf16[1,128,2048]{2,1,0:T(8,128)(2,1)} %bitcast.4) | data formatting | bytes 1048576
